TPU v7x, 32 devices: a whole 2x2x4 slice. The times are simulated.
32 devices in a mesh: wide: 16 (over z, x, core), narrow: 2 (over y).
Axes of the slice: x: 2, y: 2, z: 4, core: 2. Of those that a mesh axis runs over, the one named last changes fastest.
Arguments:
- matrix_slab: float32 [16, 262144], P(None, ('wide', 'narrow')), may hold values from -6 to 6
- row_signs: int32 [262144], P(('wide', 'narrow')), may hold values from -1 to 1, as said below
- sample_rows: int32 [32768], P(('wide', 'narrow')), may hold values from 0 to 7, as said below
Outputs:
- sketch: float32 [16, 32768], P(None, ('wide', 'narrow'))
- sketch_gram: float32 [16, 16], replicated
Inputs may be any that keep to these rules, and one draw needn't show every extreme that they name: `row_signs`: each entry is +1 or -1. `sample_rows`: entry k is the offset of the k-th sampled row inside the run of 8 rows that starts at k * 8.
All inputs are finite; a program needn't handle non-finite values.
Results may differ from a plain program's by a relative error of at most 0.00013.
Values sent between devices are 32-bit elements; how exact they have to be, the bound alone decides.
No kernel may reach another device: no remote copies, remote signals or barrier semaphores. Data moves between devices by JAX's collectives and lax.ppermute only.
A program may use at most 64 MiB of HBM per device.

v0:
```python
import functools
import math

import jax
import jax.numpy as jnp
from jax import lax
from jax.experimental import pallas as pl
from jax.experimental.pallas import tpu as pltpu
from jax.sharding import PartitionSpec as P

LANES = 128
SUBLANES = 8
AXES = ("wide", "narrow")
SPLIT_AXES = ("line", "plane", "narrow")
ORDER = ("plane", "narrow", "line")
VMEM_LIMIT = 32 * 1024 * 1024
FETCHES = 4
MESSAGE_ROWS = 6


def butterfly(values):
    values = list(values)
    apart = 1
    while apart < len(values):
        for low in range(len(values)):
            if not low & apart:
                first, second = values[low], values[low | apart]
                values[low], values[low | apart] = first + second, first - second
        apart *= 2
    return values


def sylvester(order_size):
    rows = lax.broadcasted_iota(jnp.int32, (order_size, order_size), 0)
    cols = lax.broadcasted_iota(jnp.int32, (order_size, order_size), 1)
    common = rows & cols
    parity = jnp.zeros_like(common)
    for bit_pos in range(order_size.bit_length() - 1):
        parity = parity ^ (common >> bit_pos)
    return (1 - 2 * (parity & 1)).astype(jnp.float32)


def split_dot(values, table, parts=3):
    total = None
    for _ in range(parts):
        part = values.astype(jnp.bfloat16)
        values = values - part.astype(jnp.float32)
        product = jnp.dot(part, table, preferred_element_type=jnp.float32)
        total = product if total is None else total + product
    return total


def butterfly_steps(count):
    steps = []
    apart = 1
    while apart < count:
        radix = min(8, count // apart)
        for start in range(count):
            if start // apart % radix == 0:
                steps.append((apart, [start + apart * index for index in range(radix)]))
        apart *= radix
    return steps


def fetch_blocks(x_hbm, signs_hbm, out_ref, x_ref, signs_ref, arrived):
    blocks, columns, _ = out_ref.shape
    share = blocks // FETCHES
    fetches = [pltpu.make_async_copy(signs_hbm, signs_ref, arrived.at[0])]
    for piece in range(FETCHES):
        place = (slice(None), pl.ds(piece * share * LANES, share * LANES))
        fetches.append(
            pltpu.make_async_copy(x_hbm.at[place], x_ref.at[place], arrived.at[piece + 1])
        )
    for fetch in fetches:
        fetch.start()
    table = sylvester(LANES).astype(jnp.bfloat16)
    fetches[0].wait()
    for piece in range(FETCHES):
        fetches[piece + 1].wait()
        signed = []
        for block in range(piece * share, (piece + 1) * share):
            signs = signs_ref[block : block + 1, :].astype(jnp.float32)
            signed.append(x_ref[:, block * LANES : (block + 1) * LANES] * signs)
        mixed = split_dot(jnp.concatenate(signed, axis=0), table)
        out_ref[piece * share : (piece + 1) * share] = mixed.reshape(share, columns, LANES)


def local_kernel(x_hbm, signs_hbm, out_ref, x_ref, signs_ref, arrived):
    fetch_blocks(x_hbm, signs_hbm, out_ref, x_ref, signs_ref, arrived)
    for apart, places in butterfly_steps(out_ref.shape[0]):
        for place, value in zip(places, butterfly([out_ref[p] for p in places])):
            out_ref[place] = value


def sliced_kernel(
    x_hbm, signs_hbm, samples_hbm, final_ref, out_ref, x_ref, signs_ref, samples_ref, arrived, noted
):
    note = pltpu.make_async_copy(samples_hbm, samples_ref, noted)
    note.start()
    fetch_blocks(x_hbm, signs_hbm, out_ref, x_ref, signs_ref, arrived)
    blocks, columns, _ = out_ref.shape
    slices = blocks // 2
    rows = final_ref.shape[0] // slices
    note.wait()
    samples = samples_ref[...].astype(jnp.float32)
    per_row = slices // samples.shape[0]
    for turn in range(per_row):
        shift = LANES - turn * LANES // per_row
        turned = pltpu.roll(samples, shift, 1) if turn else samples
        for index in range(turn, slices, per_row):
            tail = (index + 1) * rows - 1
            final_ref[tail : tail + 1, :] = turned[index // per_row : index // per_row + 1]
    steps = butterfly_steps(blocks)
    last = steps[-1][0]
    for apart, places in steps:
        for place, value in zip(places, butterfly([out_ref[p] for p in places])):
            if apart == last:
                start = place // 2 * rows + place % 2 * columns
                final_ref[start : start + columns, :] = value
            else:
                out_ref[place] = value


def in_vmem(count):
    return [pl.BlockSpec(memory_space=pltpu.VMEM)] * count


def in_hbm(*arrays):
    return [pltpu.with_memory_space_constraint(array, pltpu.HBM) for array in arrays]


def fetch_scratch(matrix_slab, blocks):
    return [
        pltpu.VMEM(matrix_slab.shape, jnp.float32),
        pltpu.VMEM((blocks, LANES), jnp.int32),
    ]


def local_transform(matrix_slab, row_signs):
    columns, row_count = matrix_slab.shape
    blocks = row_count // LANES
    return pl.pallas_call(
        local_kernel,
        out_shape=jax.ShapeDtypeStruct((blocks, columns, LANES), jnp.float32),
        in_specs=[pl.BlockSpec(memory_space=pltpu.HBM)] * 2,
        out_specs=in_vmem(1)[0],
        scratch_shapes=[
            *fetch_scratch(matrix_slab, blocks),
            pltpu.SemaphoreType.DMA((FETCHES + 1,)),
        ],
        compiler_params=pltpu.CompilerParams(vmem_limit_bytes=VMEM_LIMIT),
    )(*in_hbm(matrix_slab, row_signs.reshape(blocks, LANES)))


def sliced_transform(matrix_slab, row_signs, sample_rows):
    columns, row_count = matrix_slab.shape
    blocks = row_count // LANES
    samples = sample_rows.reshape(-1, LANES)
    return pl.pallas_call(
        sliced_kernel,
        out_shape=jax.ShapeDtypeStruct((blocks // 2 * (2 * columns + 1), LANES), jnp.float32),
        in_specs=[pl.BlockSpec(memory_space=pltpu.HBM)] * 3,
        out_specs=in_vmem(1)[0],
        scratch_shapes=[
            pltpu.VMEM((blocks, columns, LANES), jnp.float32),
            *fetch_scratch(matrix_slab, blocks),
            pltpu.VMEM(samples.shape, jnp.int32),
            pltpu.SemaphoreType.DMA((FETCHES + 1,)),
            pltpu.SemaphoreType.DMA(()),
        ],
        compiler_params=pltpu.CompilerParams(vmem_limit_bytes=VMEM_LIMIT),
    )(*in_hbm(matrix_slab, row_signs.reshape(blocks, LANES), samples))


def mix_kernel(run_length, scale, gram_scale, x_ref, out_ref):
    devices = out_ref.shape[0] // MESSAGE_ROWS
    rows = x_ref.shape[0] // devices
    runs = LANES // run_length
    samples = jnp.concatenate(
        [x_ref[(s + 1) * rows - 1 : (s + 1) * rows, :] for s in range(devices)], axis=0
    ).astype(jnp.bfloat16)
    run_of = lax.broadcasted_iota(jnp.int32, (LANES, 2 * LANES), 0)
    row_of = lax.broadcasted_iota(jnp.int32, (LANES, 2 * LANES), 1)
    spread = jnp.where(row_of // run_length == run_of, 1.0, 0.0).astype(jnp.bfloat16)
    offsets = jnp.dot(samples, spread, preferred_element_type=jnp.float32)
    own = lax.broadcasted_iota(jnp.int32, offsets.shape, 1) % run_length
    mask = jnp.where(offsets == own.astype(jnp.float32), scale, 0.0)
    picked = []
    for part in range(4):
        block = part // 2
        starts = [s * rows + part * SUBLANES for s in range(devices)]
        mixed = butterfly([x_ref[start : start + SUBLANES, :] for start in starts])
        picked.append(
            jnp.concatenate(
                [
                    mixed[d] * mask[d : d + 1, block * LANES : (block + 1) * LANES]
                    for d in range(devices)
                ],
                axis=0,
            )
        )
    quarter = 2 * runs
    row = lax.broadcasted_iota(jnp.int32, (4 * LANES, 2 * LANES), 0)
    lane = lax.broadcasted_iota(jnp.int32, (4 * LANES, 2 * LANES), 1)
    in_block, in_half = row // (2 * LANES), row // LANES % 2
    group = lane // quarter
    half_here = jnp.where(group >= 6, 7 - group, group % 2)
    target = in_block * runs + row % LANES // run_length
    place = jnp.where((half_here == in_half) & (lane % quarter == target), 1.0, 0.0)
    gathered = split_dot(jnp.concatenate(picked, axis=1), place.astype(jnp.bfloat16), 2)
    straight, crossed = gathered[:, :LANES], gathered[:, LANES:]
    totals = []
    for turn in range(SUBLANES):
        total = None
        for d in range(devices):
            one = straight[d * SUBLANES : (d + 1) * SUBLANES]
            two = crossed[d * SUBLANES : (d + 1) * SUBLANES]
            if turn:
                two = pltpu.roll(two, SUBLANES - turn, 0)
            total = one * two if total is None else total + one * two
        totals.append(total)
    row = lax.broadcasted_iota(jnp.int32, (LANES, 4 * LANES), 0)
    lane = lax.broadcasted_iota(jnp.int32, (LANES, 4 * LANES), 1)
    together = jnp.where(row // quarter == lane // LANES, 1.0, 0.0).astype(jnp.bfloat16)
    sums = split_dot(jnp.concatenate(totals, axis=0), together) * gram_scale
    sub = lax.broadcasted_iota(jnp.int32, (SUBLANES, LANES), 0)
    lane = lax.broadcasted_iota(jnp.int32, (SUBLANES, LANES), 1)
    first, second = [jnp.zeros((SUBLANES, LANES), jnp.float32)] * 2
    for turn in range(SUBLANES):
        here = sums[turn * SUBLANES : (turn + 1) * SUBLANES]
        quarters = [here[:, q * LANES : (q + 1) * LANES] for q in range(4)]
        mine = lane % SUBLANES == (sub + turn) % SUBLANES
        left = lane // SUBLANES % 2 == 0
        first = jnp.where(mine, jnp.where(left, quarters[0], quarters[2]), first)
        second = jnp.where(mine, jnp.where(left, quarters[3], quarters[1]), second)
    in_place = lane // (2 * SUBLANES) == sub
    gram = jnp.concatenate(
        [jnp.sum(jnp.where(in_place, part, 0.0), axis=0, keepdims=True) for part in (first, second)],
        axis=0,
    )
    half = SUBLANES // 2
    lane = lax.broadcasted_iota(jnp.int32, (half, LANES), 1)
    for d in range(devices):
        one = straight[d * SUBLANES : (d + 1) * SUBLANES]
        start = d * MESSAGE_ROWS
        out_ref[start : start + half, :] = jnp.where(lane < LANES // 2, one[:half], one[half:])
        out_ref[start + half : start + MESSAGE_ROWS, :] = gram


def mix_and_pick(received, devices, run_length, scale, gram_scale):
    return pl.pallas_call(
        functools.partial(mix_kernel, run_length, scale, gram_scale),
        out_shape=jax.ShapeDtypeStruct((devices * MESSAGE_ROWS, LANES), jnp.float32),
        in_specs=in_vmem(1),
        out_specs=in_vmem(1)[0],
        compiler_params=pltpu.CompilerParams(vmem_limit_bytes=VMEM_LIMIT),
    )(received)


def finish_kernel(x_ref, sketch_ref, gram_ref):
    sources = x_ref.shape[0] // MESSAGE_ROWS
    quarter = LANES // 4
    half_rows = SUBLANES // 2
    sub = lax.broadcasted_iota(jnp.int32, (SUBLANES, LANES), 0)
    lane = lax.broadcasted_iota(jnp.int32, (SUBLANES, LANES), 1)
    gram = None
    for start in range(0, sources, 4):
        halves = [None, None]
        for index in range(4):
            place = (start + index) * MESSAGE_ROWS
            tail = x_ref[place + half_rows : place + MESSAGE_ROWS, :]
            gram = tail if gram is None else gram + tail
            piece = x_ref[place : place + half_rows, :]
            piece = jnp.concatenate([piece, piece], axis=0)
            piece = jnp.where(sub < half_rows, piece, pltpu.roll(piece, LANES // 2, 1))
            for half in range(2):
                shift = (index - half) % 4 * quarter
                moved = pltpu.roll(piece, shift, 1) if shift else piece
                if halves[half] is None:
                    halves[half] = moved
                else:
                    halves[half] = jnp.where(lane // quarter == index, moved, halves[half])
        for half in range(2):
            sketch_ref[
                half * SUBLANES : (half + 1) * SUBLANES, start * quarter : (start + 4) * quarter
            ] = halves[half]
    columns = gram_ref.shape[0]
    for half in range(2):
        for row in range(SUBLANES):
            line = gram[half : half + 1]
            line = pltpu.roll(line, LANES - row * columns, 1) if row else line
            gram_ref[half * SUBLANES + row : half * SUBLANES + row + 1, :] = line[:, :columns]


def finish(received, columns, sample_count):
    return pl.pallas_call(
        finish_kernel,
        out_shape=(
            jax.ShapeDtypeStruct((columns, sample_count), jnp.float32),
            jax.ShapeDtypeStruct((columns, columns), jnp.float32),
        ),
        in_specs=[pl.BlockSpec(memory_space=pltpu.VMEM)],
        out_specs=(pl.BlockSpec(memory_space=pltpu.VMEM),) * 2,
        compiler_params=pltpu.CompilerParams(vmem_limit_bytes=VMEM_LIMIT),
    )(received)


def exchange(values, axes):
    return lax.all_to_all(values, axes, split_axis=0, concat_axis=0, tiled=True)


def general_shards(matrix_slab, row_signs, sample_rows):
    columns, row_count = matrix_slab.shape
    sample_count = sample_rows.shape[0]
    devices = lax.axis_size("wide") * lax.axis_size("narrow")
    run_length = row_count // sample_count
    slice_rows = row_count // devices
    slice_runs = slice_rows // run_length
    values = jnp.swapaxes(local_transform(matrix_slab, row_signs), 0, 1)
    values = values.reshape(columns, devices, slice_rows)
    received = exchange(jnp.swapaxes(values, 0, 1), AXES)
    offsets = exchange(sample_rows.reshape(devices, slice_runs), AXES)
    mixed = jnp.einsum("ds,scr->dcr", sylvester(devices), received, precision=lax.Precision.HIGHEST)
    mixed = mixed.reshape(devices, columns, slice_runs, run_length)
    chosen = offsets[:, None, :, None] == lax.iota(jnp.int32, run_length)
    picked = jnp.sum(jnp.where(chosen, mixed, 0.0), axis=3)
    picked = picked * jnp.float32(1.0 / math.sqrt(row_count * devices))
    gram = jnp.einsum("dck,dek->ce", picked, picked, precision=lax.Precision.HIGHEST)
    gram = gram / jnp.float32(sample_count * devices)
    grams = jnp.broadcast_to(gram[None], (devices, columns, columns))
    back = exchange(jnp.concatenate([picked, grams], axis=2), AXES)
    sketch = jnp.swapaxes(back[:, :, :slice_runs], 0, 1).reshape(columns, devices * slice_runs)
    return sketch, jnp.sum(back[:, :, slice_runs:], axis=0)


def sliced_shards(matrix_slab, row_signs, sample_rows):
    columns, row_count = matrix_slab.shape
    sample_count = sample_rows.shape[0]
    devices = lax.axis_size(ORDER)
    run_length = row_count // sample_count
    sent = sliced_transform(matrix_slab, row_signs, sample_rows)
    received = exchange(sent.reshape(devices, -1), ORDER).reshape(sent.shape)
    scale = 1.0 / math.sqrt(row_count * devices)
    gram_scale = 1.0 / (sample_count * devices)
    picked = mix_and_pick(received, devices, run_length, scale, gram_scale)
    returned = exchange(picked.reshape(devices, -1), ORDER).reshape(picked.shape)
    return finish(returned, columns, sample_count)


def solution(mesh):
    wide, narrow = mesh.shape["wide"], mesh.shape["narrow"]
    axes, function = AXES, general_shards
    if wide * narrow == 32 and wide % 4 == 0:
        axes, function = SPLIT_AXES, sliced_shards
        mesh = jax.sharding.Mesh(mesh.devices.reshape(4, wide // 4, narrow), axes)
    in_specs = (P(None, axes), P(axes), P(axes))
    out_specs = (P(None, axes), P())
    return jax.shard_map(function, mesh=mesh, in_specs=in_specs, out_specs=out_specs, check_vma=False)
```

profile of v0, /device:TPU:0, one launch (start us, length us, event | category | flops | bytes accessed | tf_op | source)
XLA Modules:
  0.0 37.2 jit_solution(1373164497911314602)
XLA Ops:
  0.6 2.0 %shard_map.50 = f32[1056,128]{1,0:T(8,128)S(1)} custom-call(f32[16,8192]{1,0:T(8,128)} %x_hbm.1, s32[64,128]{1,0:T(8,128)} %bitcast.10, s32[8,128]{1,0:T(8,128)} %bitcast.11), custom_call_target="tpu_custom_call" | custom-call | tf_op jit(solution)/shard_map/pallas_call | solution.py:159
  2.7 23.2 %all_to_all.18 = f32[32,1,4224]{2,1,0:T(1,128)S(1)} all-to-all(f32[32,1,4224]{2,1,0:T(1,128)S(1)} %bitcast.7), channel_id=1, replica_groups=mesh['line'=4,'plane'=4,'narrow'=2] {'plane','narrow','line'}, dimensions={0} | all-to-all | bytes 1081344 | tf_op jit(solution)/shard_map/all_to_all | solution.py:309
  25.9 0.9 %shard_map.51 = f32[192,128]{1,0:T(8,128)S(1)} custom-call(f32[1056,128]{1,0:T(8,128)S(1)} %bitcast.6), custom_call_target="tpu_custom_call" | custom-call | tf_op jit(solution)/shard_map/pallas_call | solution.py:251
  26.8 9.6 %all_to_all.19 = f32[32,1,768]{2,1,0:T(1,128)S(1)} all-to-all(f32[32,1,768]{2,1,0:T(1,128)S(1)} %bitcast.9), channel_id=1, replica_groups=mesh['line'=4,'plane'=4,'narrow'=2] {'plane','narrow','line'}, dimensions={0} | all-to-all | bytes 196608 | tf_op jit(solution)/shard_map/all_to_all | solution.py:309
  36.4 0.8 %shard_map.52 = (f32[16,1024]{1,0:T(8,128)}, f32[16,16]{1,0:T(8,128)}) custom-call(f32[192,128]{1,0:T(8,128)S(1)} %bitcast.8), custom_call_target="tpu_custom_call" | custom-call | tf_op jit(solution)/shard_map/pallas_call | solution.py:296
where the time goes:
time: 37.4 us; the launch traced here: 37.2 us
  blocking collectives  32.8 us (88%)
  Pallas kernels  3.79 us (10%)
  between operations  0.65 us (2%)
    all_to_all x2, blocking collectives, exchange(): return lax.all_to_all(values, axes, split_axis=0, concat_axis=0, tiled=True)  32.8 us
    pallas_call x1, Pallas kernels, sliced_transform(): pl.pallas_call(sliced_kernel, out_shape=jax.ShapeDtypeStruct((blocks // 2...  2.03 us
    pallas_call x1, Pallas kernels, mix_and_pick(): pl.pallas_call(functools.partial(mix_kernel, run_length, scale, gram_scal...  0.92 us
    pallas_call x1, Pallas kernels, finish(): pl.pallas_call(finish_kernel, out_shape=(jax.ShapeDtypeStruct((columns, s...  0.83 us

commit v1 on v0

--- a/solution.py
+++ b/solution.py
@@ -14,7 +14,6 @@
 SPLIT_AXES = ("line", "plane", "narrow")
 ORDER = ("plane", "narrow", "line")
 VMEM_LIMIT = 32 * 1024 * 1024
-FETCHES = 4
 MESSAGE_ROWS = 6
 
 
@@ -64,25 +63,24 @@
 
 def fetch_blocks(x_hbm, signs_hbm, out_ref, x_ref, signs_ref, arrived):
     blocks, columns, _ = out_ref.shape
-    share = blocks // FETCHES
     fetches = [pltpu.make_async_copy(signs_hbm, signs_ref, arrived.at[0])]
-    for piece in range(FETCHES):
-        place = (slice(None), pl.ds(piece * share * LANES, share * LANES))
+    places = [pl.ds(start, SUBLANES) for start in range(0, columns, SUBLANES)]
+    for index, place in enumerate(places):
         fetches.append(
-            pltpu.make_async_copy(x_hbm.at[place], x_ref.at[place], arrived.at[piece + 1])
+            pltpu.make_async_copy(x_hbm.at[place], x_ref.at[place], arrived.at[index + 1])
         )
     for fetch in fetches:
         fetch.start()
     table = sylvester(LANES).astype(jnp.bfloat16)
     fetches[0].wait()
-    for piece in range(FETCHES):
-        fetches[piece + 1].wait()
+    for index, place in enumerate(places):
+        fetches[index + 1].wait()
         signed = []
-        for block in range(piece * share, (piece + 1) * share):
+        for block in range(blocks):
             signs = signs_ref[block : block + 1, :].astype(jnp.float32)
-            signed.append(x_ref[:, block * LANES : (block + 1) * LANES] * signs)
+            signed.append(x_ref[place, block * LANES : (block + 1) * LANES] * signs)
         mixed = split_dot(jnp.concatenate(signed, axis=0), table)
-        out_ref[piece * share : (piece + 1) * share] = mixed.reshape(share, columns, LANES)
+        out_ref[:, place, :] = mixed.reshape(blocks, SUBLANES, LANES)
 
 
 def local_kernel(x_hbm, signs_hbm, out_ref, x_ref, signs_ref, arrived):
@@ -146,7 +144,7 @@
         out_specs=in_vmem(1)[0],
         scratch_shapes=[
             *fetch_scratch(matrix_slab, blocks),
-            pltpu.SemaphoreType.DMA((FETCHES + 1,)),
+            pltpu.SemaphoreType.DMA((columns // SUBLANES + 1,)),
         ],
         compiler_params=pltpu.CompilerParams(vmem_limit_bytes=VMEM_LIMIT),
     )(*in_hbm(matrix_slab, row_signs.reshape(blocks, LANES)))
@@ -165,7 +163,7 @@
             pltpu.VMEM((blocks, columns, LANES), jnp.float32),
             *fetch_scratch(matrix_slab, blocks),
             pltpu.VMEM(samples.shape, jnp.int32),
-            pltpu.SemaphoreType.DMA((FETCHES + 1,)),
+            pltpu.SemaphoreType.DMA((columns // SUBLANES + 1,)),
             pltpu.SemaphoreType.DMA(()),
         ],
         compiler_params=pltpu.CompilerParams(vmem_limit_bytes=VMEM_LIMIT),
@@ -200,17 +198,23 @@
             )
         )
     quarter = 2 * runs
-    row = lax.broadcasted_iota(jnp.int32, (4 * LANES, 2 * LANES), 0)
-    lane = lax.broadcasted_iota(jnp.int32, (4 * LANES, 2 * LANES), 1)
-    in_block, in_half = row // (2 * LANES), row // LANES % 2
+    row = lax.broadcasted_iota(jnp.int32, (LANES, LANES), 0)
+    lane = lax.broadcasted_iota(jnp.int32, (LANES, LANES), 1)
+    pattern = jnp.where(row // run_length == lane % runs, 1.0, 0.0)
+    lane = lax.broadcasted_iota(jnp.int32, (1, LANES), 1)
     group = lane // quarter
-    half_here = jnp.where(group >= 6, 7 - group, group % 2)
-    target = in_block * runs + row % LANES // run_length
-    place = jnp.where((half_here == in_half) & (lane % quarter == target), 1.0, 0.0)
-    gathered = split_dot(jnp.concatenate(picked, axis=1), place.astype(jnp.bfloat16), 2)
+    place = []
+    for part in range(4):
+        block, half = part // 2, part % 2
+        here = lane // runs % 2 == block
+        sides = [group % 2, jnp.where(group < 2, group, 3 - group)]
+        masks = [jnp.where(here & (side == half), 1.0, 0.0) for side in sides]
+        place.append(jnp.concatenate([(pattern * mask).astype(jnp.bfloat16) for mask in masks], axis=1))
+    gathered = split_dot(jnp.concatenate(picked, axis=1), jnp.concatenate(place, axis=0), 2)
     straight, crossed = gathered[:, :LANES], gathered[:, LANES:]
+    turns = SUBLANES // 2 + 1
     totals = []
-    for turn in range(SUBLANES):
+    for turn in range(turns):
         total = None
         for d in range(devices):
             one = straight[d * SUBLANES : (d + 1) * SUBLANES]
@@ -219,16 +223,18 @@
                 two = pltpu.roll(two, SUBLANES - turn, 0)
             total = one * two if total is None else total + one * two
         totals.append(total)
-    row = lax.broadcasted_iota(jnp.int32, (LANES, 4 * LANES), 0)
-    lane = lax.broadcasted_iota(jnp.int32, (LANES, 4 * LANES), 1)
-    together = jnp.where(row // quarter == lane // LANES, 1.0, 0.0).astype(jnp.bfloat16)
-    sums = split_dot(jnp.concatenate(totals, axis=0), together) * gram_scale
+    from_quarter = row // quarter
+    together = [jnp.where(from_quarter == q, 1.0, 0.0).astype(jnp.bfloat16) for q in range(4)]
+    sums = split_dot(jnp.concatenate(totals, axis=0), jnp.concatenate(together, axis=1)) * gram_scale
     sub = lax.broadcasted_iota(jnp.int32, (SUBLANES, LANES), 0)
     lane = lax.broadcasted_iota(jnp.int32, (SUBLANES, LANES), 1)
     first, second = [jnp.zeros((SUBLANES, LANES), jnp.float32)] * 2
     for turn in range(SUBLANES):
-        here = sums[turn * SUBLANES : (turn + 1) * SUBLANES]
+        known = min(turn, SUBLANES - turn)
+        here = sums[known * SUBLANES : (known + 1) * SUBLANES]
         quarters = [here[:, q * LANES : (q + 1) * LANES] for q in range(4)]
+        if known != turn:
+            quarters = [pltpu.roll(quarters[q], known, 0) for q in (0, 1, 3, 2)]
         mine = lane % SUBLANES == (sub + turn) % SUBLANES
         left = lane // SUBLANES % 2 == 0
         first = jnp.where(mine, jnp.where(left, quarters[0], quarters[2]), first)

time: 37.4 us -> 37 us (0.989)
  Pallas kernels: 3.79 us -> 3.37 us
where the time goes in v1:
time: 37 us; the launch traced here: 36.8 us
  blocking collectives  32.8 us (89%)
  Pallas kernels  3.37 us (9%)
  between operations  0.65 us (2%)
    all_to_all x2, blocking collectives, exchange(): return lax.all_to_all(values, axes, split_axis=0, concat_axis=0, tiled=True)  32.8 us
    pallas_call x1, Pallas kernels, sliced_transform(): pl.pallas_call(sliced_kernel, out_shape=jax.ShapeDtypeStruct((blocks // 2...  1.79 us
    pallas_call x1, Pallas kernels, finish(): pl.pallas_call(finish_kernel, out_shape=(jax.ShapeDtypeStruct((columns, s...  0.83 us
    pallas_call x1, Pallas kernels, mix_and_pick(): pl.pallas_call(functools.partial(mix_kernel, run_length, scale, gram_scal...  0.74 us

profile of v1, /device:TPU:0, one launch (start us, length us, event | category | flops | bytes accessed | tf_op | source)
XLA Modules:
  0.0 36.8 jit_solution(13873204811845293173)
XLA Ops:
  0.6 1.8 %shard_map.50 = f32[1056,128]{1,0:T(8,128)S(1)} custom-call(f32[16,8192]{1,0:T(8,128)} %x_hbm.1, s32[64,128]{1,0:T(8,128)} %bitcast.10, s32[8,128]{1,0:T(8,128)} %bitcast.11), custom_call_target="tpu_custom_call" | custom-call | tf_op jit(solution)/shard_map/pallas_call | solution.py:157
  2.4 23.2 %all_to_all.18 = f32[32,1,4224]{2,1,0:T(1,128)S(1)} all-to-all(f32[32,1,4224]{2,1,0:T(1,128)S(1)} %bitcast.7), channel_id=1, replica_groups=mesh['line'=4,'plane'=4,'narrow'=2] {'plane','narrow','line'}, dimensions={0} | all-to-all | bytes 1081344 | tf_op jit(solution)/shard_map/all_to_all | solution.py:315
  25.6 0.7 %shard_map.51 = f32[192,128]{1,0:T(8,128)S(1)} custom-call(f32[1056,128]{1,0:T(8,128)S(1)} %bitcast.6), custom_call_target="tpu_custom_call" | custom-call | tf_op jit(solution)/shard_map/pallas_call | solution.py:257
  26.4 9.6 %all_to_all.19 = f32[32,1,768]{2,1,0:T(1,128)S(1)} all-to-all(f32[32,1,768]{2,1,0:T(1,128)S(1)} %bitcast.9), channel_id=1, replica_groups=mesh['line'=4,'plane'=4,'narrow'=2] {'plane','narrow','line'}, dimensions={0} | all-to-all | bytes 196608 | tf_op jit(solution)/shard_map/all_to_all | solution.py:315
  36.0 0.8 %shard_map.52 = (f32[16,1024]{1,0:T(8,128)}, f32[16,16]{1,0:T(8,128)}) custom-call(f32[192,128]{1,0:T(8,128)S(1)} %bitcast.8), custom_call_target="tpu_custom_call" | custom-call | tf_op jit(solution)/shard_map/pallas_call | solution.py:302

commit v2 on v1

--- a/solution.py
+++ b/solution.py
@@ -51,7 +51,7 @@
 
 def butterfly_steps(count):
     steps = []
-    apart = 1
+    apart = 2
     while apart < count:
         radix = min(8, count // apart)
         for start in range(count):
@@ -71,16 +71,19 @@
         )
     for fetch in fetches:
         fetch.start()
-    table = sylvester(LANES).astype(jnp.bfloat16)
+    table = sylvester(2 * LANES).astype(jnp.bfloat16)
     fetches[0].wait()
+    signs = signs_ref[...].astype(jnp.float32)
     for index, place in enumerate(places):
         fetches[index + 1].wait()
         signed = []
+        for block in range(0, blocks, 2):
+            pair = jnp.concatenate([signs[block : block + 1], signs[block + 1 : block + 2]], axis=1)
+            signed.append(x_ref[place, block * LANES : (block + 2) * LANES] * pair)
+        mixed = split_dot(jnp.concatenate(signed, axis=0), table)
         for block in range(blocks):
-            signs = signs_ref[block : block + 1, :].astype(jnp.float32)
-            signed.append(x_ref[place, block * LANES : (block + 1) * LANES] * signs)
-        mixed = split_dot(jnp.concatenate(signed, axis=0), table)
-        out_ref[:, place, :] = mixed.reshape(blocks, SUBLANES, LANES)
+            rows = slice(block // 2 * SUBLANES, (block // 2 + 1) * SUBLANES)
+            out_ref[block, place, :] = mixed[rows, block % 2 * LANES : (block % 2 + 1) * LANES]
 
 
 def local_kernel(x_hbm, signs_hbm, out_ref, x_ref, signs_ref, arrived):

time: 37 us -> 37 us (level)
  no operation moved by 1% of the time
where the time goes in v2:
time: 37 us; the launch traced here: 36.8 us
  blocking collectives  32.8 us (89%)
  Pallas kernels  3.39 us (9%)
  between operations  0.65 us (2%)
    all_to_all x2, blocking collectives, exchange(): return lax.all_to_all(values, axes, split_axis=0, concat_axis=0, tiled=True)  32.8 us
    pallas_call x1, Pallas kernels, sliced_transform(): pl.pallas_call(sliced_kernel, out_shape=jax.ShapeDtypeStruct((blocks // 2...  1.81 us
    pallas_call x1, Pallas kernels, finish(): pl.pallas_call(finish_kernel, out_shape=(jax.ShapeDtypeStruct((columns, s...  0.83 us
    pallas_call x1, Pallas kernels, mix_and_pick(): pl.pallas_call(functools.partial(mix_kernel, run_length, scale, gram_scal...  0.74 us

profile of v2, /device:TPU:0, one launch (start us, length us, event | category | flops | bytes accessed | tf_op | source)
XLA Modules:
  0.0 36.8 jit_solution(11950872419107589780)
XLA Ops:
  0.6 1.8 %shard_map.50 = f32[1056,128]{1,0:T(8,128)S(1)} custom-call(f32[16,8192]{1,0:T(8,128)} %x_hbm.1, s32[64,128]{1,0:T(8,128)} %bitcast.10, s32[8,128]{1,0:T(8,128)} %bitcast.11), custom_call_target="tpu_custom_call" | custom-call | tf_op jit(solution)/shard_map/pallas_call | solution.py:160
  2.4 23.2 %all_to_all.18 = f32[32,1,4224]{2,1,0:T(1,128)S(1)} all-to-all(f32[32,1,4224]{2,1,0:T(1,128)S(1)} %bitcast.7), channel_id=1, replica_groups=mesh['line'=4,'plane'=4,'narrow'=2] {'plane','narrow','line'}, dimensions={0} | all-to-all | bytes 1081344 | tf_op jit(solution)/shard_map/all_to_all | solution.py:318
  25.6 0.7 %shard_map.51 = f32[192,128]{1,0:T(8,128)S(1)} custom-call(f32[1056,128]{1,0:T(8,128)S(1)} %bitcast.6), custom_call_target="tpu_custom_call" | custom-call | tf_op jit(solution)/shard_map/pallas_call | solution.py:260
  26.4 9.6 %all_to_all.19 = f32[32,1,768]{2,1,0:T(1,128)S(1)} all-to-all(f32[32,1,768]{2,1,0:T(1,128)S(1)} %bitcast.9), channel_id=1, replica_groups=mesh['line'=4,'plane'=4,'narrow'=2] {'plane','narrow','line'}, dimensions={0} | all-to-all | bytes 196608 | tf_op jit(solution)/shard_map/all_to_all | solution.py:318
  36.0 0.8 %shard_map.52 = (f32[16,1024]{1,0:T(8,128)}, f32[16,16]{1,0:T(8,128)}) custom-call(f32[192,128]{1,0:T(8,128)S(1)} %bitcast.8), custom_call_target="tpu_custom_call" | custom-call | tf_op jit(solution)/shard_map/pallas_call | solution.py:305

commit v3 on v1

--- a/solution.py
+++ b/solution.py
@@ -170,17 +170,51 @@
     )(*in_hbm(matrix_slab, row_signs.reshape(blocks, LANES), samples))
 
 
-def mix_kernel(run_length, scale, gram_scale, x_ref, out_ref):
+def table_kernel(run_length, spread_ref, place_ref, together_ref):
+    runs = LANES // run_length
+    run_of = lax.broadcasted_iota(jnp.int32, (LANES, 2 * LANES), 0)
+    row_of = lax.broadcasted_iota(jnp.int32, (LANES, 2 * LANES), 1)
+    spread_ref[...] = jnp.where(row_of // run_length == run_of, 1.0, 0.0).astype(jnp.bfloat16)
+    quarter = 2 * runs
+    row = lax.broadcasted_iota(jnp.int32, (LANES, LANES), 0)
+    lane = lax.broadcasted_iota(jnp.int32, (LANES, LANES), 1)
+    pattern = jnp.where(row // run_length == lane % runs, 1.0, 0.0)
+    lane = lax.broadcasted_iota(jnp.int32, (1, LANES), 1)
+    group = lane // quarter
+    place = []
+    for part in range(4):
+        block, half = part // 2, part % 2
+        here = lane // runs % 2 == block
+        sides = [group % 2, jnp.where(group < 2, group, 3 - group)]
+        masks = [jnp.where(here & (side == half), 1.0, 0.0) for side in sides]
+        place.append(jnp.concatenate([(pattern * mask).astype(jnp.bfloat16) for mask in masks], axis=1))
+    place_ref[...] = jnp.concatenate(place, axis=0)
+    from_quarter = row // quarter
+    together = [jnp.where(from_quarter == q, 1.0, 0.0).astype(jnp.bfloat16) for q in range(4)]
+    together_ref[...] = jnp.concatenate(together, axis=1)
+
+
+def tables(run_length):
+    return pl.pallas_call(
+        functools.partial(table_kernel, run_length),
+        out_shape=tuple(
+            jax.ShapeDtypeStruct(shape, jnp.bfloat16)
+            for shape in ((LANES, 2 * LANES), (4 * LANES, 2 * LANES), (LANES, 4 * LANES))
+        ),
+        out_specs=tuple(in_vmem(3)),
+        compiler_params=pltpu.CompilerParams(vmem_limit_bytes=VMEM_LIMIT),
+    )()
+
+
+def mix_kernel(
+    run_length, scale, gram_scale, x_ref, spread_ref, place_ref, together_ref, out_ref
+):
     devices = out_ref.shape[0] // MESSAGE_ROWS
     rows = x_ref.shape[0] // devices
-    runs = LANES // run_length
     samples = jnp.concatenate(
         [x_ref[(s + 1) * rows - 1 : (s + 1) * rows, :] for s in range(devices)], axis=0
     ).astype(jnp.bfloat16)
-    run_of = lax.broadcasted_iota(jnp.int32, (LANES, 2 * LANES), 0)
-    row_of = lax.broadcasted_iota(jnp.int32, (LANES, 2 * LANES), 1)
-    spread = jnp.where(row_of // run_length == run_of, 1.0, 0.0).astype(jnp.bfloat16)
-    offsets = jnp.dot(samples, spread, preferred_element_type=jnp.float32)
+    offsets = jnp.dot(samples, spread_ref[...], preferred_element_type=jnp.float32)
     own = lax.broadcasted_iota(jnp.int32, offsets.shape, 1) % run_length
     mask = jnp.where(offsets == own.astype(jnp.float32), scale, 0.0)
     picked = []
@@ -197,20 +231,7 @@
                 axis=0,
             )
         )
-    quarter = 2 * runs
-    row = lax.broadcasted_iota(jnp.int32, (LANES, LANES), 0)
-    lane = lax.broadcasted_iota(jnp.int32, (LANES, LANES), 1)
-    pattern = jnp.where(row // run_length == lane % runs, 1.0, 0.0)
-    lane = lax.broadcasted_iota(jnp.int32, (1, LANES), 1)
-    group = lane // quarter
-    place = []
-    for part in range(4):
-        block, half = part // 2, part % 2
-        here = lane // runs % 2 == block
-        sides = [group % 2, jnp.where(group < 2, group, 3 - group)]
-        masks = [jnp.where(here & (side == half), 1.0, 0.0) for side in sides]
-        place.append(jnp.concatenate([(pattern * mask).astype(jnp.bfloat16) for mask in masks], axis=1))
-    gathered = split_dot(jnp.concatenate(picked, axis=1), jnp.concatenate(place, axis=0), 2)
+    gathered = split_dot(jnp.concatenate(picked, axis=1), place_ref[...], 2)
     straight, crossed = gathered[:, :LANES], gathered[:, LANES:]
     turns = SUBLANES // 2 + 1
     totals = []
@@ -223,9 +244,7 @@
                 two = pltpu.roll(two, SUBLANES - turn, 0)
             total = one * two if total is None else total + one * two
         totals.append(total)
-    from_quarter = row // quarter
-    together = [jnp.where(from_quarter == q, 1.0, 0.0).astype(jnp.bfloat16) for q in range(4)]
-    sums = split_dot(jnp.concatenate(totals, axis=0), jnp.concatenate(together, axis=1)) * gram_scale
+    sums = split_dot(jnp.concatenate(totals, axis=0), together_ref[...]) * gram_scale
     sub = lax.broadcasted_iota(jnp.int32, (SUBLANES, LANES), 0)
     lane = lax.broadcasted_iota(jnp.int32, (SUBLANES, LANES), 1)
     first, second = [jnp.zeros((SUBLANES, LANES), jnp.float32)] * 2
@@ -257,10 +276,10 @@
     return pl.pallas_call(
         functools.partial(mix_kernel, run_length, scale, gram_scale),
         out_shape=jax.ShapeDtypeStruct((devices * MESSAGE_ROWS, LANES), jnp.float32),
-        in_specs=in_vmem(1),
+        in_specs=in_vmem(4),
         out_specs=in_vmem(1)[0],
         compiler_params=pltpu.CompilerParams(vmem_limit_bytes=VMEM_LIMIT),
-    )(received)
+    )(received, *tables(run_length))
 
 
 def finish_kernel(x_ref, sketch_ref, gram_ref):

time: 37 us -> 38 us (1.027)
  blocking collectives: 32.8 us -> 9.62 us
  waiting for transfers between devices: 0 us -> 16 us
  starting transfers between devices: 0 us -> 7.3 us
  Pallas kernels: 3.37 us -> 4.22 us
    all_to_all x2 -> x1, blocking collectives: 32.8 us -> 9.62 us  [exchange(): return lax.all_to_all(values, axes, split_axis=0, concat_axis=0, tiled=True)]
    all_to_all x0 -> x1, waiting for transfers between devices: none -> 16 us  [exchange(): return lax.all_to_all(values, axes, split_axis=0, concat_axis=0, tiled=True)]
    all_to_all x0 -> x1, starting transfers between devices: none -> 7.3 us  [exchange(): return lax.all_to_all(values, axes, split_axis=0, concat_axis=0, tiled=True)]
    pallas_call x1, Pallas kernels: 1.79 us -> 2.58 us  [sliced_transform(): pl.pallas_call(sliced_kernel, out_shape=jax.ShapeDtypeStruct((blocks // 2...]
  transfers between devices with their start and end apart: 0 -> 1, of which waited for: 0 -> 1; matrix products, arithmetic and copies ran while one was open for 0% -> 0% of each run, Pallas kernels for 0% -> 0%
where the time goes in v3:
time: 38 us; the launch traced here: 37.8 us
  waiting for transfers between devices  16 us (42%)
  blocking collectives  9.62 us (25%)
  starting transfers between devices  7.3 us (19%)
  Pallas kernels  4.22 us (11%)
  between operations  0.66 us (2%)
    all_to_all x1, waiting for transfers between devices, exchange(): return lax.all_to_all(values, axes, split_axis=0, concat_axis=0, tiled=True)  16 us
    all_to_all x1, blocking collectives, exchange(): return lax.all_to_all(values, axes, split_axis=0, concat_axis=0, tiled=True)  9.62 us
    all_to_all x1, starting transfers between devices, exchange(): return lax.all_to_all(values, axes, split_axis=0, concat_axis=0, tiled=True)  7.3 us
    pallas_call x1, Pallas kernels, sliced_transform(): pl.pallas_call(sliced_kernel, out_shape=jax.ShapeDtypeStruct((blocks // 2...  2.58 us
    pallas_call x1, Pallas kernels, finish(): pl.pallas_call(finish_kernel, out_shape=(jax.ShapeDtypeStruct((columns, s...  0.83 us
  transfers between devices with their start and end apart: 1, of which 1 were waited for; matrix products, arithmetic and copies ran while one was open for 0% of the time, Pallas kernels for 0%

profile of v3, /device:TPU:0, one launch (start us, length us, event | category | flops | bytes accessed | tf_op | source)
XLA Modules:
  0.0 37.8 jit_solution(18294750822454871859)
XLA Ops:
  0.6 2.6 %shard_map.50 = f32[1056,128]{1,0:T(8,128)} custom-call(f32[16,8192]{1,0:T(8,128)} %x_hbm.1, s32[64,128]{1,0:T(8,128)} %bitcast.9, s32[8,128]{1,0:T(8,128)} %bitcast.10), custom_call_target="tpu_custom_call" | custom-call | tf_op jit(solution)/shard_map/pallas_call | solution.py:157
  3.2 7.3 %all-to-all-start = ((f32[32,1,4224]{2,1,0:T(1,128)}), f32[32,1,4224]{2,1,0:T(1,128)S(1)}, u32[]{:S(2)}, u32[]{:S(2)}) async-start(f32[32,1,4224]{2,1,0:T(1,128)} %bitcast.2), calls=%async_computation | async-start | bytes 1081344 | tf_op jit(solution)/shard_map/all_to_all | solution.py:334
  10.5 0.1 shard_map.51
  10.6 16.0 %all-to-all-done = f32[32,1,4224]{2,1,0:T(1,128)S(1)} async-done(((f32[32,1,4224]{2,1,0:T(1,128)}), f32[32,1,4224]{2,1,0:T(1,128)S(1)}, u32[]{:S(2)}, u32[]{:S(2)}) %all-to-all-start) | async-done | bytes 540704 | tf_op jit(solution)/shard_map/all_to_all | solution.py:334
  26.6 0.7 %shard_map.52 = f32[192,128]{1,0:T(8,128)S(1)} custom-call(f32[1056,128]{1,0:T(8,128)S(1)} %bitcast.6, bf16[128,256]{1,0:T(8,128)(2,1)S(1)} %get-tuple-element.5.spread_ref, bf16[512,256]{1,0:T(8,128)(2,1)S(1)} %get-tuple-element.6.place_ref, bf16[128,512]{1,0:T(8,128)(2,1)S(1)} %get-tuple-element.7.together_ref), custom_call_target="tpu_custom_call" | custom-call | tf_op jit(solution)/shard_map/pallas_call | solution.py:276
  27.4 9.6 %all_to_all.18 = f32[32,1,768]{2,1,0:T(1,128)S(1)} all-to-all(f32[32,1,768]{2,1,0:T(1,128)S(1)} %bitcast.7), channel_id=1, replica_groups=mesh['line'=4,'plane'=4,'narrow'=2] {'plane','narrow','line'}, dimensions={0} | all-to-all | bytes 196608 | tf_op jit(solution)/shard_map/all_to_all | solution.py:334
  37.0 0.8 %shard_map.53 = (f32[16,1024]{1,0:T(8,128)}, f32[16,16]{1,0:T(8,128)}) custom-call(f32[192,128]{1,0:T(8,128)S(1)} %bitcast.8), custom_call_target="tpu_custom_call" | custom-call | tf_op jit(solution)/shard_map/pallas_call | solution.py:321
Async XLA Ops:
  3.2 23.4 %all-to-all-start = ((f32[32,1,4224]{2,1,0:T(1,128)}), f32[32,1,4224]{2,1,0:T(1,128)S(1)}, u32[]{:S(2)}, u32[]{:S(2)}) async-start(f32[32,1,4224]{2,1,0:T(1,128)} %bitcast.2), calls=%async_computation | async-start | bytes 1081344 | tf_op jit(solution)/shard_map/all_to_all | solution.py:334

commit v4 on v1

--- a/solution.py
+++ b/solution.py
@@ -63,24 +63,22 @@
 
 def fetch_blocks(x_hbm, signs_hbm, out_ref, x_ref, signs_ref, arrived):
     blocks, columns, _ = out_ref.shape
-    fetches = [pltpu.make_async_copy(signs_hbm, signs_ref, arrived.at[0])]
-    places = [pl.ds(start, SUBLANES) for start in range(0, columns, SUBLANES)]
-    for index, place in enumerate(places):
-        fetches.append(
-            pltpu.make_async_copy(x_hbm.at[place], x_ref.at[place], arrived.at[index + 1])
-        )
+    fetches = [
+        pltpu.make_async_copy(x_hbm, x_ref, arrived.at[0]),
+        pltpu.make_async_copy(signs_hbm, signs_ref, arrived.at[1]),
+    ]
     for fetch in fetches:
         fetch.start()
     table = sylvester(LANES).astype(jnp.bfloat16)
-    fetches[0].wait()
-    for index, place in enumerate(places):
-        fetches[index + 1].wait()
-        signed = []
-        for block in range(blocks):
-            signs = signs_ref[block : block + 1, :].astype(jnp.float32)
-            signed.append(x_ref[place, block * LANES : (block + 1) * LANES] * signs)
-        mixed = split_dot(jnp.concatenate(signed, axis=0), table)
-        out_ref[:, place, :] = mixed.reshape(blocks, SUBLANES, LANES)
+    for fetch in fetches:
+        fetch.wait()
+    signs = signs_ref[...].astype(jnp.float32)
+    signed = [
+        x_ref[:, block * LANES : (block + 1) * LANES] * signs[block : block + 1]
+        for block in range(blocks)
+    ]
+    mixed = split_dot(jnp.concatenate(signed, axis=0), table)
+    out_ref[...] = mixed.reshape(blocks, columns, LANES)
 
 
 def local_kernel(x_hbm, signs_hbm, out_ref, x_ref, signs_ref, arrived):
@@ -144,7 +142,7 @@
         out_specs=in_vmem(1)[0],
         scratch_shapes=[
             *fetch_scratch(matrix_slab, blocks),
-            pltpu.SemaphoreType.DMA((columns // SUBLANES + 1,)),
+            pltpu.SemaphoreType.DMA((2,)),
         ],
         compiler_params=pltpu.CompilerParams(vmem_limit_bytes=VMEM_LIMIT),
     )(*in_hbm(matrix_slab, row_signs.reshape(blocks, LANES)))
@@ -163,7 +161,7 @@
             pltpu.VMEM((blocks, columns, LANES), jnp.float32),
             *fetch_scratch(matrix_slab, blocks),
             pltpu.VMEM(samples.shape, jnp.int32),
-            pltpu.SemaphoreType.DMA((columns // SUBLANES + 1,)),
+            pltpu.SemaphoreType.DMA((2,)),
             pltpu.SemaphoreType.DMA(()),
         ],
         compiler_params=pltpu.CompilerParams(vmem_limit_bytes=VMEM_LIMIT),

time: 37 us -> 36.8 us (level)
  no operation moved by 1% of the time
where the time goes in v4:
time: 36.8 us; the launch traced here: 36.6 us
  blocking collectives  32.8 us (89%)
  Pallas kernels  3.14 us (9%)
  between operations  0.65 us (2%)
    all_to_all x2, blocking collectives, exchange(): return lax.all_to_all(values, axes, split_axis=0, concat_axis=0, tiled=True)  32.8 us
    pallas_call x1, Pallas kernels, sliced_transform(): pl.pallas_call(sliced_kernel, out_shape=jax.ShapeDtypeStruct((blocks // 2...  1.56 us
    pallas_call x1, Pallas kernels, finish(): pl.pallas_call(finish_kernel, out_shape=(jax.ShapeDtypeStruct((columns, s...  0.83 us
    pallas_call x1, Pallas kernels, mix_and_pick(): pl.pallas_call(functools.partial(mix_kernel, run_length, scale, gram_scal...  0.74 us

profile of v4, /device:TPU:0, one launch (start us, length us, event | category | flops | bytes accessed | tf_op | source)
XLA Modules:
  0.0 36.6 jit_solution(3298110794722916825)
XLA Ops:
  0.6 1.6 %shard_map.50 = f32[1056,128]{1,0:T(8,128)S(1)} custom-call(f32[16,8192]{1,0:T(8,128)} %x_hbm.1, s32[64,128]{1,0:T(8,128)} %bitcast.10, s32[8,128]{1,0:T(8,128)} %bitcast.11), custom_call_target="tpu_custom_call" | custom-call | tf_op jit(solution)/shard_map/pallas_call | solution.py:155
  2.2 23.2 %all_to_all.18 = f32[32,1,4224]{2,1,0:T(1,128)S(1)} all-to-all(f32[32,1,4224]{2,1,0:T(1,128)S(1)} %bitcast.7), channel_id=1, replica_groups=mesh['line'=4,'plane'=4,'narrow'=2] {'plane','narrow','line'}, dimensions={0} | all-to-all | bytes 1081344 | tf_op jit(solution)/shard_map/all_to_all | solution.py:313
  25.4 0.7 %shard_map.51 = f32[192,128]{1,0:T(8,128)S(1)} custom-call(f32[1056,128]{1,0:T(8,128)S(1)} %bitcast.6), custom_call_target="tpu_custom_call" | custom-call | tf_op jit(solution)/shard_map/pallas_call | solution.py:255
  26.1 9.6 %all_to_all.19 = f32[32,1,768]{2,1,0:T(1,128)S(1)} all-to-all(f32[32,1,768]{2,1,0:T(1,128)S(1)} %bitcast.9), channel_id=1, replica_groups=mesh['line'=4,'plane'=4,'narrow'=2] {'plane','narrow','line'}, dimensions={0} | all-to-all | bytes 196608 | tf_op jit(solution)/shard_map/all_to_all | solution.py:313
  35.8 0.8 %shard_map.52 = (f32[16,1024]{1,0:T(8,128)}, f32[16,16]{1,0:T(8,128)}) custom-call(f32[192,128]{1,0:T(8,128)S(1)} %bitcast.8), custom_call_target="tpu_custom_call" | custom-call | tf_op jit(solution)/shard_map/pallas_call | solution.py:300

commit v5 on v4

--- a/solution.py
+++ b/solution.py
@@ -51,7 +51,7 @@
 
 def butterfly_steps(count):
     steps = []
-    apart = 1
+    apart = 2
     while apart < count:
         radix = min(8, count // apart)
         for start in range(count):
@@ -69,16 +69,18 @@
     ]
     for fetch in fetches:
         fetch.start()
-    table = sylvester(LANES).astype(jnp.bfloat16)
+    table = sylvester(2 * LANES).astype(jnp.bfloat16)
     for fetch in fetches:
         fetch.wait()
     signs = signs_ref[...].astype(jnp.float32)
-    signed = [
-        x_ref[:, block * LANES : (block + 1) * LANES] * signs[block : block + 1]
-        for block in range(blocks)
-    ]
+    signed = []
+    for block in range(0, blocks, 2):
+        pair = jnp.concatenate([signs[block : block + 1], signs[block + 1 : block + 2]], axis=1)
+        signed.append(x_ref[:, block * LANES : (block + 2) * LANES] * pair)
     mixed = split_dot(jnp.concatenate(signed, axis=0), table)
-    out_ref[...] = mixed.reshape(blocks, columns, LANES)
+    for block in range(blocks):
+        rows = slice(block // 2 * columns, (block // 2 + 1) * columns)
+        out_ref[block] = mixed[rows, block % 2 * LANES : (block % 2 + 1) * LANES]
 
 
 def local_kernel(x_hbm, signs_hbm, out_ref, x_ref, signs_ref, arrived):

time: 36.8 us -> 36.8 us (level)
  no operation moved by 1% of the time
where the time goes in v5:
time: 36.8 us; the launch traced here: 36.6 us
  blocking collectives  32.8 us (89%)
  Pallas kernels  3.14 us (9%)
  between operations  0.65 us (2%)
    all_to_all x2, blocking collectives, exchange(): return lax.all_to_all(values, axes, split_axis=0, concat_axis=0, tiled=True)  32.8 us
    pallas_call x1, Pallas kernels, sliced_transform(): pl.pallas_call(sliced_kernel, out_shape=jax.ShapeDtypeStruct((blocks // 2...  1.56 us
    pallas_call x1, Pallas kernels, finish(): pl.pallas_call(finish_kernel, out_shape=(jax.ShapeDtypeStruct((columns, s...  0.83 us
    pallas_call x1, Pallas kernels, mix_and_pick(): pl.pallas_call(functools.partial(mix_kernel, run_length, scale, gram_scal...  0.74 us

profile of v5, /device:TPU:0, one launch (start us, length us, event | category | flops | bytes accessed | tf_op | source)
XLA Modules:
  0.0 36.6 jit_solution(4425051300519820737)
XLA Ops:
  0.6 1.6 %shard_map.50 = f32[1056,128]{1,0:T(8,128)S(1)} custom-call(f32[16,8192]{1,0:T(8,128)} %x_hbm.1, s32[64,128]{1,0:T(8,128)} %bitcast.10, s32[8,128]{1,0:T(8,128)} %bitcast.11), custom_call_target="tpu_custom_call" | custom-call | tf_op jit(solution)/shard_map/pallas_call | solution.py:157
  2.2 23.2 %all_to_all.18 = f32[32,1,4224]{2,1,0:T(1,128)S(1)} all-to-all(f32[32,1,4224]{2,1,0:T(1,128)S(1)} %bitcast.7), channel_id=1, replica_groups=mesh['line'=4,'plane'=4,'narrow'=2] {'plane','narrow','line'}, dimensions={0} | all-to-all | bytes 1081344 | tf_op jit(solution)/shard_map/all_to_all | solution.py:315
  25.4 0.7 %shard_map.51 = f32[192,128]{1,0:T(8,128)S(1)} custom-call(f32[1056,128]{1,0:T(8,128)S(1)} %bitcast.6), custom_call_target="tpu_custom_call" | custom-call | tf_op jit(solution)/shard_map/pallas_call | solution.py:257
  26.1 9.6 %all_to_all.19 = f32[32,1,768]{2,1,0:T(1,128)S(1)} all-to-all(f32[32,1,768]{2,1,0:T(1,128)S(1)} %bitcast.9), channel_id=1, replica_groups=mesh['line'=4,'plane'=4,'narrow'=2] {'plane','narrow','line'}, dimensions={0} | all-to-all | bytes 196608 | tf_op jit(solution)/shard_map/all_to_all | solution.py:315
  35.8 0.8 %shard_map.52 = (f32[16,1024]{1,0:T(8,128)}, f32[16,16]{1,0:T(8,128)}) custom-call(f32[192,128]{1,0:T(8,128)S(1)} %bitcast.8), custom_call_target="tpu_custom_call" | custom-call | tf_op jit(solution)/shard_map/pallas_call | solution.py:302

commit v6 on v4

--- a/solution.py
+++ b/solution.py
@@ -237,7 +237,7 @@
         left = lane // SUBLANES % 2 == 0
         first = jnp.where(mine, jnp.where(left, quarters[0], quarters[2]), first)
         second = jnp.where(mine, jnp.where(left, quarters[3], quarters[1]), second)
-    in_place = lane // (2 * SUBLANES) == sub
+    in_place = lane // (2 * SUBLANES) == (SUBLANES - sub) % SUBLANES
     gram = jnp.concatenate(
         [jnp.sum(jnp.where(in_place, part, 0.0), axis=0, keepdims=True) for part in (first, second)],
         axis=0,
@@ -267,33 +267,32 @@
     half_rows = SUBLANES // 2
     sub = lax.broadcasted_iota(jnp.int32, (SUBLANES, LANES), 0)
     lane = lax.broadcasted_iota(jnp.int32, (SUBLANES, LANES), 1)
+    even = lane // quarter % 2 == 0
+    stays = (sub < half_rows) == (lane < LANES // 2)
     gram = None
     for start in range(0, sources, 4):
-        halves = [None, None]
+        rows = []
         for index in range(4):
             place = (start + index) * MESSAGE_ROWS
             tail = x_ref[place + half_rows : place + MESSAGE_ROWS, :]
             gram = tail if gram is None else gram + tail
-            piece = x_ref[place : place + half_rows, :]
-            piece = jnp.concatenate([piece, piece], axis=0)
-            piece = jnp.where(sub < half_rows, piece, pltpu.roll(piece, LANES // 2, 1))
-            for half in range(2):
-                shift = (index - half) % 4 * quarter
-                moved = pltpu.roll(piece, shift, 1) if shift else piece
-                if halves[half] is None:
-                    halves[half] = moved
-                else:
-                    halves[half] = jnp.where(lane // quarter == index, moved, halves[half])
-        for half in range(2):
+            rows.append(x_ref[place : place + half_rows, :])
+        one = jnp.concatenate([rows[0], rows[2]], axis=0)
+        two = jnp.concatenate([rows[1], rows[3]], axis=0)
+        halves = [
+            jnp.where(even, one, pltpu.roll(two, quarter, 1)),
+            jnp.where(even, pltpu.roll(one, LANES - quarter, 1), two),
+        ]
+        for half, value in enumerate(halves):
+            crossed = pltpu.roll(pltpu.roll(value, half_rows, 0), LANES // 2, 1)
             sketch_ref[
                 half * SUBLANES : (half + 1) * SUBLANES, start * quarter : (start + 4) * quarter
-            ] = halves[half]
+            ] = jnp.where(stays, value, crossed)
     columns = gram_ref.shape[0]
     for half in range(2):
-        for row in range(SUBLANES):
-            line = gram[half : half + 1]
-            line = pltpu.roll(line, LANES - row * columns, 1) if row else line
-            gram_ref[half * SUBLANES + row : half * SUBLANES + row + 1, :] = line[:, :columns]
+        lines = jnp.broadcast_to(gram[half : half + 1], (SUBLANES, LANES))
+        turned = pltpu.roll(lines, 0, 1, stride=columns, stride_axis=0)
+        gram_ref[half * SUBLANES : (half + 1) * SUBLANES, :] = turned[:, :columns]
 
 
 def finish(received, columns, sample_count):

time: 36.8 us -> 36.7 us (level)
  no operation moved by 1% of the time
where the time goes in v6:
time: 36.7 us; the launch traced here: 36.5 us
  blocking collectives  32.8 us (89%)
  Pallas kernels  3.09 us (8%)
  between operations  0.65 us (2%)
    all_to_all x2, blocking collectives, exchange(): return lax.all_to_all(values, axes, split_axis=0, concat_axis=0, tiled=True)  32.8 us
    pallas_call x1, Pallas kernels, sliced_transform(): pl.pallas_call(sliced_kernel, out_shape=jax.ShapeDtypeStruct((blocks // 2...  1.56 us
    pallas_call x1, Pallas kernels, finish(): pl.pallas_call(finish_kernel, out_shape=(jax.ShapeDtypeStruct((columns, s...  0.79 us
    pallas_call x1, Pallas kernels, mix_and_pick(): pl.pallas_call(functools.partial(mix_kernel, run_length, scale, gram_scal...  0.74 us

profile of v6, /device:TPU:0, one launch (start us, length us, event | category | flops | bytes accessed | tf_op | source)
XLA Modules:
  0.0 36.5 jit_solution(4994048524665736920)
XLA Ops:
  0.6 1.6 %shard_map.50 = f32[1056,128]{1,0:T(8,128)S(1)} custom-call(f32[16,8192]{1,0:T(8,128)} %x_hbm.1, s32[64,128]{1,0:T(8,128)} %bitcast.10, s32[8,128]{1,0:T(8,128)} %bitcast.11), custom_call_target="tpu_custom_call" | custom-call | tf_op jit(solution)/shard_map/pallas_call | solution.py:155
  2.2 23.2 %all_to_all.18 = f32[32,1,4224]{2,1,0:T(1,128)S(1)} all-to-all(f32[32,1,4224]{2,1,0:T(1,128)S(1)} %bitcast.7), channel_id=1, replica_groups=mesh['line'=4,'plane'=4,'narrow'=2] {'plane','narrow','line'}, dimensions={0} | all-to-all | bytes 1081344 | tf_op jit(solution)/shard_map/all_to_all | solution.py:312
  25.4 0.7 %shard_map.51 = f32[192,128]{1,0:T(8,128)S(1)} custom-call(f32[1056,128]{1,0:T(8,128)S(1)} %bitcast.6), custom_call_target="tpu_custom_call" | custom-call | tf_op jit(solution)/shard_map/pallas_call | solution.py:255
  26.1 9.6 %all_to_all.19 = f32[32,1,768]{2,1,0:T(1,128)S(1)} all-to-all(f32[32,1,768]{2,1,0:T(1,128)S(1)} %bitcast.9), channel_id=1, replica_groups=mesh['line'=4,'plane'=4,'narrow'=2] {'plane','narrow','line'}, dimensions={0} | all-to-all | bytes 196608 | tf_op jit(solution)/shard_map/all_to_all | solution.py:312
  35.8 0.8 %shard_map.52 = (f32[16,1024]{1,0:T(8,128)}, f32[16,16]{1,0:T(8,128)}) custom-call(f32[192,128]{1,0:T(8,128)S(1)} %bitcast.8), custom_call_target="tpu_custom_call" | custom-call | tf_op jit(solution)/shard_map/pallas_call | solution.py:299

commit v7 on v6

--- a/solution.py
+++ b/solution.py
@@ -61,13 +61,13 @@
     return steps
 
 
-def fetch_blocks(x_hbm, signs_hbm, out_ref, x_ref, signs_ref, arrived):
+def fetch_blocks(x_hbm, signs_hbm, out_ref, x_ref, signs_ref, arrived, *others):
     blocks, columns, _ = out_ref.shape
     fetches = [
         pltpu.make_async_copy(x_hbm, x_ref, arrived.at[0]),
         pltpu.make_async_copy(signs_hbm, signs_ref, arrived.at[1]),
     ]
-    for fetch in fetches:
+    for fetch in (*fetches, *others):
         fetch.start()
     table = sylvester(LANES).astype(jnp.bfloat16)
     for fetch in fetches:
@@ -92,8 +92,7 @@
     x_hbm, signs_hbm, samples_hbm, final_ref, out_ref, x_ref, signs_ref, samples_ref, arrived, noted
 ):
     note = pltpu.make_async_copy(samples_hbm, samples_ref, noted)
-    note.start()
-    fetch_blocks(x_hbm, signs_hbm, out_ref, x_ref, signs_ref, arrived)
+    fetch_blocks(x_hbm, signs_hbm, out_ref, x_ref, signs_ref, arrived, note)
     blocks, columns, _ = out_ref.shape
     slices = blocks // 2
     rows = final_ref.shape[0] // slices
@@ -223,7 +222,8 @@
         totals.append(total)
     from_quarter = row // quarter
     together = [jnp.where(from_quarter == q, 1.0, 0.0).astype(jnp.bfloat16) for q in range(4)]
-    sums = split_dot(jnp.concatenate(totals, axis=0), jnp.concatenate(together, axis=1)) * gram_scale
+    sums = split_dot(jnp.concatenate(totals, axis=0), jnp.concatenate(together, axis=1), 2)
+    sums = sums * gram_scale
     sub = lax.broadcasted_iota(jnp.int32, (SUBLANES, LANES), 0)
     lane = lax.broadcasted_iota(jnp.int32, (SUBLANES, LANES), 1)
     first, second = [jnp.zeros((SUBLANES, LANES), jnp.float32)] * 2

time: 36.7 us -> 36.7 us (level)
  no operation moved by 1% of the time
where the time goes in v7:
time: 36.7 us; the launch traced here: 36.5 us
  blocking collectives  32.8 us (89%)
  Pallas kernels  3.04 us (8%)
  between operations  0.65 us (2%)
    all_to_all x2, blocking collectives, exchange(): return lax.all_to_all(values, axes, split_axis=0, concat_axis=0, tiled=True)  32.8 us
    pallas_call x1, Pallas kernels, sliced_transform(): pl.pallas_call(sliced_kernel, out_shape=jax.ShapeDtypeStruct((blocks // 2...  1.56 us
    pallas_call x1, Pallas kernels, finish(): pl.pallas_call(finish_kernel, out_shape=(jax.ShapeDtypeStruct((columns, s...  0.79 us

profile of v7, /device:TPU:0, one launch (start us, length us, event | category | flops | bytes accessed | tf_op | source)
XLA Modules:
  0.0 36.5 jit_solution(1532210280318134658)
XLA Ops:
  0.6 1.6 %shard_map.50 = f32[1056,128]{1,0:T(8,128)S(1)} custom-call(f32[16,8192]{1,0:T(8,128)} %x_hbm.1, s32[64,128]{1,0:T(8,128)} %bitcast.10, s32[8,128]{1,0:T(8,128)} %bitcast.11), custom_call_target="tpu_custom_call" | custom-call | tf_op jit(solution)/shard_map/pallas_call | solution.py:154
  2.2 23.2 %all_to_all.18 = f32[32,1,4224]{2,1,0:T(1,128)S(1)} all-to-all(f32[32,1,4224]{2,1,0:T(1,128)S(1)} %bitcast.7), channel_id=1, replica_groups=mesh['line'=4,'plane'=4,'narrow'=2] {'plane','narrow','line'}, dimensions={0} | all-to-all | bytes 1081344 | tf_op jit(solution)/shard_map/all_to_all | solution.py:312
  25.4 0.7 %shard_map.51 = f32[192,128]{1,0:T(8,128)S(1)} custom-call(f32[1056,128]{1,0:T(8,128)S(1)} %bitcast.6), custom_call_target="tpu_custom_call" | custom-call | tf_op jit(solution)/shard_map/pallas_call | solution.py:255
  26.1 9.6 %all_to_all.19 = f32[32,1,768]{2,1,0:T(1,128)S(1)} all-to-all(f32[32,1,768]{2,1,0:T(1,128)S(1)} %bitcast.9), channel_id=1, replica_groups=mesh['line'=4,'plane'=4,'narrow'=2] {'plane','narrow','line'}, dimensions={0} | all-to-all | bytes 196608 | tf_op jit(solution)/shard_map/all_to_all | solution.py:312
  35.7 0.8 %shard_map.52 = (f32[16,1024]{1,0:T(8,128)}, f32[16,16]{1,0:T(8,128)}) custom-call(f32[192,128]{1,0:T(8,128)S(1)} %bitcast.8), custom_call_target="tpu_custom_call" | custom-call | tf_op jit(solution)/shard_map/pallas_call | solution.py:299

commit v8 on v7

--- a/solution.py
+++ b/solution.py
@@ -40,13 +40,15 @@
 
 
 def split_dot(values, table, parts=3):
-    total = None
+    pieces = []
     for _ in range(parts):
-        part = values.astype(jnp.bfloat16)
-        values = values - part.astype(jnp.float32)
-        product = jnp.dot(part, table, preferred_element_type=jnp.float32)
-        total = product if total is None else total + product
-    return total
+        pieces.append(values.astype(jnp.bfloat16))
+        values = values - pieces[-1].astype(jnp.float32)
+    return jnp.dot(
+        jnp.concatenate(pieces, axis=1),
+        jnp.concatenate([table] * parts, axis=0),
+        preferred_element_type=jnp.float32,
+    )
 
 
 def butterfly_steps(count):

time: 36.7 us -> 36.6 us (level)
  no operation moved by 1% of the time
where the time goes in v8:
time: 36.6 us; the launch traced here: 36.5 us
  blocking collectives  32.8 us (90%)
  Pallas kernels  3.02 us (8%)
  between operations  0.65 us (2%)
    all_to_all x2, blocking collectives, exchange(): return lax.all_to_all(values, axes, split_axis=0, concat_axis=0, tiled=True)  32.8 us
    pallas_call x1, Pallas kernels, sliced_transform(): pl.pallas_call(sliced_kernel, out_shape=jax.ShapeDtypeStruct((blocks // 2...  1.56 us
    pallas_call x1, Pallas kernels, finish(): pl.pallas_call(finish_kernel, out_shape=(jax.ShapeDtypeStruct((columns, s...  0.79 us

profile of v8, /device:TPU:0, one launch (start us, length us, event | category | flops | bytes accessed | tf_op | source)
XLA Modules:
  0.0 36.5 jit_solution(3555888556869385900)
XLA Ops:
  0.6 1.6 %shard_map.50 = f32[1056,128]{1,0:T(8,128)S(1)} custom-call(f32[16,8192]{1,0:T(8,128)} %x_hbm.1, s32[64,128]{1,0:T(8,128)} %bitcast.10, s32[8,128]{1,0:T(8,128)} %bitcast.11), custom_call_target="tpu_custom_call" | custom-call | tf_op jit(solution)/shard_map/pallas_call | solution.py:156
  2.2 23.2 %all_to_all.18 = f32[32,1,4224]{2,1,0:T(1,128)S(1)} all-to-all(f32[32,1,4224]{2,1,0:T(1,128)S(1)} %bitcast.7), channel_id=1, replica_groups=mesh['line'=4,'plane'=4,'narrow'=2] {'plane','narrow','line'}, dimensions={0} | all-to-all | bytes 1081344 | tf_op jit(solution)/shard_map/all_to_all | solution.py:314
  25.4 0.7 %shard_map.51 = f32[192,128]{1,0:T(8,128)S(1)} custom-call(f32[1056,128]{1,0:T(8,128)S(1)} %bitcast.6), custom_call_target="tpu_custom_call" | custom-call | tf_op jit(solution)/shard_map/pallas_call | solution.py:257
  26.1 9.6 %all_to_all.19 = f32[32,1,768]{2,1,0:T(1,128)S(1)} all-to-all(f32[32,1,768]{2,1,0:T(1,128)S(1)} %bitcast.9), channel_id=1, replica_groups=mesh['line'=4,'plane'=4,'narrow'=2] {'plane','narrow','line'}, dimensions={0} | all-to-all | bytes 196608 | tf_op jit(solution)/shard_map/all_to_all | solution.py:314
  35.7 0.8 %shard_map.52 = (f32[16,1024]{1,0:T(8,128)}, f32[16,16]{1,0:T(8,128)}) custom-call(f32[192,128]{1,0:T(8,128)S(1)} %bitcast.8), custom_call_target="tpu_custom_call" | custom-call | tf_op jit(solution)/shard_map/pallas_call | solution.py:301

commit v9 on v8

--- a/solution.py
+++ b/solution.py
@@ -63,8 +63,8 @@
     return steps
 
 
-def fetch_blocks(x_hbm, signs_hbm, out_ref, x_ref, signs_ref, arrived, *others):
-    blocks, columns, _ = out_ref.shape
+def fetch_blocks(x_hbm, signs_hbm, x_ref, signs_ref, arrived, *others):
+    columns, blocks = x_ref.shape[0], x_ref.shape[1] // LANES
     fetches = [
         pltpu.make_async_copy(x_hbm, x_ref, arrived.at[0]),
         pltpu.make_async_copy(signs_hbm, signs_ref, arrived.at[1]),
@@ -80,13 +80,14 @@
         for block in range(blocks)
     ]
     mixed = split_dot(jnp.concatenate(signed, axis=0), table)
-    out_ref[...] = mixed.reshape(blocks, columns, LANES)
+    return [mixed[block * columns : (block + 1) * columns] for block in range(blocks)]
 
 
 def local_kernel(x_hbm, signs_hbm, out_ref, x_ref, signs_ref, arrived):
-    fetch_blocks(x_hbm, signs_hbm, out_ref, x_ref, signs_ref, arrived)
+    mixed = fetch_blocks(x_hbm, signs_hbm, x_ref, signs_ref, arrived)
     for apart, places in butterfly_steps(out_ref.shape[0]):
-        for place, value in zip(places, butterfly([out_ref[p] for p in places])):
+        values = [mixed[p] if apart == 1 else out_ref[p] for p in places]
+        for place, value in zip(places, butterfly(values)):
             out_ref[place] = value
 
 
@@ -94,7 +95,7 @@
     x_hbm, signs_hbm, samples_hbm, final_ref, out_ref, x_ref, signs_ref, samples_ref, arrived, noted
 ):
     note = pltpu.make_async_copy(samples_hbm, samples_ref, noted)
-    fetch_blocks(x_hbm, signs_hbm, out_ref, x_ref, signs_ref, arrived, note)
+    mixed = fetch_blocks(x_hbm, signs_hbm, x_ref, signs_ref, arrived, note)
     blocks, columns, _ = out_ref.shape
     slices = blocks // 2
     rows = final_ref.shape[0] // slices
@@ -110,7 +111,8 @@
     steps = butterfly_steps(blocks)
     last = steps[-1][0]
     for apart, places in steps:
-        for place, value in zip(places, butterfly([out_ref[p] for p in places])):
+        values = [mixed[p] if apart == 1 else out_ref[p] for p in places]
+        for place, value in zip(places, butterfly(values)):
             if apart == last:
                 start = place // 2 * rows + place % 2 * columns
                 final_ref[start : start + columns, :] = value

time: 36.6 us -> 36.6 us (level)
  no operation moved by 1% of the time
where the time goes in v9:
time: 36.6 us; the launch traced here: 36.5 us
  blocking collectives  32.8 us (90%)
  Pallas kernels  3.02 us (8%)
  between operations  0.65 us (2%)
    all_to_all x2, blocking collectives, exchange(): return lax.all_to_all(values, axes, split_axis=0, concat_axis=0, tiled=True)  32.8 us
    pallas_call x1, Pallas kernels, sliced_transform(): pl.pallas_call(sliced_kernel, out_shape=jax.ShapeDtypeStruct((blocks // 2...  1.56 us
    pallas_call x1, Pallas kernels, finish(): pl.pallas_call(finish_kernel, out_shape=(jax.ShapeDtypeStruct((columns, s...  0.79 us

profile of v9, /device:TPU:0, one launch (start us, length us, event | category | flops | bytes accessed | tf_op | source)
XLA Modules:
  0.0 36.5 jit_solution(3555888556869385900)
XLA Ops:
  0.6 1.6 %shard_map.50 = f32[1056,128]{1,0:T(8,128)S(1)} custom-call(f32[16,8192]{1,0:T(8,128)} %x_hbm.1, s32[64,128]{1,0:T(8,128)} %bitcast.10, s32[8,128]{1,0:T(8,128)} %bitcast.11), custom_call_target="tpu_custom_call" | custom-call | tf_op jit(solution)/shard_map/pallas_call | solution.py:158
  2.2 23.2 %all_to_all.18 = f32[32,1,4224]{2,1,0:T(1,128)S(1)} all-to-all(f32[32,1,4224]{2,1,0:T(1,128)S(1)} %bitcast.7), channel_id=1, replica_groups=mesh['line'=4,'plane'=4,'narrow'=2] {'plane','narrow','line'}, dimensions={0} | all-to-all | bytes 1081344 | tf_op jit(solution)/shard_map/all_to_all | solution.py:316
  25.4 0.7 %shard_map.51 = f32[192,128]{1,0:T(8,128)S(1)} custom-call(f32[1056,128]{1,0:T(8,128)S(1)} %bitcast.6), custom_call_target="tpu_custom_call" | custom-call | tf_op jit(solution)/shard_map/pallas_call | solution.py:259
  26.1 9.6 %all_to_all.19 = f32[32,1,768]{2,1,0:T(1,128)S(1)} all-to-all(f32[32,1,768]{2,1,0:T(1,128)S(1)} %bitcast.9), channel_id=1, replica_groups=mesh['line'=4,'plane'=4,'narrow'=2] {'plane','narrow','line'}, dimensions={0} | all-to-all | bytes 196608 | tf_op jit(solution)/shard_map/all_to_all | solution.py:316
  35.7 0.8 %shard_map.52 = (f32[16,1024]{1,0:T(8,128)}, f32[16,16]{1,0:T(8,128)}) custom-call(f32[192,128]{1,0:T(8,128)S(1)} %bitcast.8), custom_call_target="tpu_custom_call" | custom-call | tf_op jit(solution)/shard_map/pallas_call | solution.py:303

commit v10 on v9

--- a/solution.py
+++ b/solution.py
@@ -63,7 +63,7 @@
     return steps
 
 
-def fetch_blocks(x_hbm, signs_hbm, x_ref, signs_ref, arrived, *others):
+def fetch_blocks(x_hbm, signs_hbm, x_ref, signs_ref, spread_ref, arrived, *others):
     columns, blocks = x_ref.shape[0], x_ref.shape[1] // LANES
     fetches = [
         pltpu.make_async_copy(x_hbm, x_ref, arrived.at[0]),
@@ -72,19 +72,22 @@
     for fetch in (*fetches, *others):
         fetch.start()
     table = sylvester(LANES).astype(jnp.bfloat16)
-    for fetch in fetches:
-        fetch.wait()
+    fetches[1].wait()
     signs = signs_ref[...].astype(jnp.float32)
-    signed = [
-        x_ref[:, block * LANES : (block + 1) * LANES] * signs[block : block + 1]
-        for block in range(blocks)
-    ]
+    for block in range(blocks):
+        spread_ref[block] = jnp.broadcast_to(signs[block : block + 1], (SUBLANES, LANES))
+    fetches[0].wait()
+    signed = []
+    for block in range(blocks):
+        for start in range(0, columns, SUBLANES):
+            place = (slice(start, start + SUBLANES), slice(block * LANES, (block + 1) * LANES))
+            signed.append(x_ref[place] * spread_ref[block])
     mixed = split_dot(jnp.concatenate(signed, axis=0), table)
     return [mixed[block * columns : (block + 1) * columns] for block in range(blocks)]
 
 
-def local_kernel(x_hbm, signs_hbm, out_ref, x_ref, signs_ref, arrived):
-    mixed = fetch_blocks(x_hbm, signs_hbm, x_ref, signs_ref, arrived)
+def local_kernel(x_hbm, signs_hbm, out_ref, x_ref, signs_ref, spread_ref, arrived):
+    mixed = fetch_blocks(x_hbm, signs_hbm, x_ref, signs_ref, spread_ref, arrived)
     for apart, places in butterfly_steps(out_ref.shape[0]):
         values = [mixed[p] if apart == 1 else out_ref[p] for p in places]
         for place, value in zip(places, butterfly(values)):
@@ -92,10 +95,10 @@
 
 
 def sliced_kernel(
-    x_hbm, signs_hbm, samples_hbm, final_ref, out_ref, x_ref, signs_ref, samples_ref, arrived, noted
+    x_hbm, signs_hbm, samples_hbm, final_ref, out_ref, x_ref, signs_ref, spread_ref, samples_ref, arrived, noted
 ):
     note = pltpu.make_async_copy(samples_hbm, samples_ref, noted)
-    mixed = fetch_blocks(x_hbm, signs_hbm, x_ref, signs_ref, arrived, note)
+    mixed = fetch_blocks(x_hbm, signs_hbm, x_ref, signs_ref, spread_ref, arrived, note)
     blocks, columns, _ = out_ref.shape
     slices = blocks // 2
     rows = final_ref.shape[0] // slices
@@ -132,6 +135,7 @@
     return [
         pltpu.VMEM(matrix_slab.shape, jnp.float32),
         pltpu.VMEM((blocks, LANES), jnp.int32),
+        pltpu.VMEM((blocks, SUBLANES, LANES), jnp.float32),
     ]
 
 

time: 36.6 us -> 36.6 us (level)
  no operation moved by 1% of the time
where the time goes in v10:
time: 36.6 us; the launch traced here: 36.5 us
  blocking collectives  32.8 us (90%)
  Pallas kernels  3.02 us (8%)
  between operations  0.65 us (2%)
    all_to_all x2, blocking collectives, exchange(): return lax.all_to_all(values, axes, split_axis=0, concat_axis=0, tiled=True)  32.8 us
    pallas_call x1, Pallas kernels, sliced_transform(): pl.pallas_call(sliced_kernel, out_shape=jax.ShapeDtypeStruct((blocks // 2...  1.57 us
    pallas_call x1, Pallas kernels, finish(): pl.pallas_call(finish_kernel, out_shape=(jax.ShapeDtypeStruct((columns, s...  0.79 us

profile of v10, /device:TPU:0, one launch (start us, length us, event | category | flops | bytes accessed | tf_op | source)
XLA Modules:
  0.0 36.5 jit_solution(9352649035720683460)
XLA Ops:
  0.6 1.6 %shard_map.50 = f32[1056,128]{1,0:T(8,128)S(1)} custom-call(f32[16,8192]{1,0:T(8,128)} %x_hbm.1, s32[64,128]{1,0:T(8,128)} %bitcast.10, s32[8,128]{1,0:T(8,128)} %bitcast.11), custom_call_target="tpu_custom_call" | custom-call | tf_op jit(solution)/shard_map/pallas_call | solution.py:162
  2.2 23.2 %all_to_all.18 = f32[32,1,4224]{2,1,0:T(1,128)S(1)} all-to-all(f32[32,1,4224]{2,1,0:T(1,128)S(1)} %bitcast.7), channel_id=1, replica_groups=mesh['line'=4,'plane'=4,'narrow'=2] {'plane','narrow','line'}, dimensions={0} | all-to-all | bytes 1081344 | tf_op jit(solution)/shard_map/all_to_all | solution.py:320
  25.4 0.7 %shard_map.51 = f32[192,128]{1,0:T(8,128)S(1)} custom-call(f32[1056,128]{1,0:T(8,128)S(1)} %bitcast.6), custom_call_target="tpu_custom_call" | custom-call | tf_op jit(solution)/shard_map/pallas_call | solution.py:263
  26.1 9.6 %all_to_all.19 = f32[32,1,768]{2,1,0:T(1,128)S(1)} all-to-all(f32[32,1,768]{2,1,0:T(1,128)S(1)} %bitcast.9), channel_id=1, replica_groups=mesh['line'=4,'plane'=4,'narrow'=2] {'plane','narrow','line'}, dimensions={0} | all-to-all | bytes 196608 | tf_op jit(solution)/shard_map/all_to_all | solution.py:320
  35.7 0.8 %shard_map.52 = (f32[16,1024]{1,0:T(8,128)}, f32[16,16]{1,0:T(8,128)}) custom-call(f32[192,128]{1,0:T(8,128)S(1)} %bitcast.8), custom_call_target="tpu_custom_call" | custom-call | tf_op jit(solution)/shard_map/pallas_call | solution.py:307

commit v11 on v9

--- a/solution.py
+++ b/solution.py
@@ -12,7 +12,7 @@
 SUBLANES = 8
 AXES = ("wide", "narrow")
 SPLIT_AXES = ("line", "plane", "narrow")
-ORDER = ("plane", "narrow", "line")
+ORDER = ("plane", "line", "narrow")
 VMEM_LIMIT = 32 * 1024 * 1024
 MESSAGE_ROWS = 6
 

time: 36.6 us -> 37.3 us (1.019)
  blocking collectives: 32.8 us -> 33.4 us
    all_to_all x2, blocking collectives: 32.8 us -> 33.4 us  [exchange(): return lax.all_to_all(values, axes, split_axis=0, concat_axis=0, tiled=True)]
where the time goes in v11:
time: 37.3 us; the launch traced here: 37.1 us
  blocking collectives  33.4 us (90%)
  Pallas kernels  3.02 us (8%)
  between operations  0.65 us (2%)
    all_to_all x2, blocking collectives, exchange(): return lax.all_to_all(values, axes, split_axis=0, concat_axis=0, tiled=True)  33.4 us
    pallas_call x1, Pallas kernels, sliced_transform(): pl.pallas_call(sliced_kernel, out_shape=jax.ShapeDtypeStruct((blocks // 2...  1.56 us
    pallas_call x1, Pallas kernels, finish(): pl.pallas_call(finish_kernel, out_shape=(jax.ShapeDtypeStruct((columns, s...  0.79 us

profile of v11, /device:TPU:0, one launch (start us, length us, event | category | flops | bytes accessed | tf_op | source)
XLA Modules:
  0.0 37.1 jit_solution(14428082070467445581)
XLA Ops:
  0.6 1.6 %shard_map.50 = f32[1056,128]{1,0:T(8,128)S(1)} custom-call(f32[16,8192]{1,0:T(8,128)} %x_hbm.1, s32[64,128]{1,0:T(8,128)} %bitcast.10, s32[8,128]{1,0:T(8,128)} %bitcast.11), custom_call_target="tpu_custom_call" | custom-call | tf_op jit(solution)/shard_map/pallas_call | solution.py:158
  2.2 23.8 %all_to_all.18 = f32[32,1,4224]{2,1,0:T(1,128)S(1)} all-to-all(f32[32,1,4224]{2,1,0:T(1,128)S(1)} %bitcast.7), channel_id=1, replica_groups=mesh['line'=4,'plane'=4,'narrow'=2] {'plane','line','narrow'}, dimensions={0} | all-to-all | bytes 1081344 | tf_op jit(solution)/shard_map/all_to_all | solution.py:316
  26.0 0.7 %shard_map.51 = f32[192,128]{1,0:T(8,128)S(1)} custom-call(f32[1056,128]{1,0:T(8,128)S(1)} %bitcast.6), custom_call_target="tpu_custom_call" | custom-call | tf_op jit(solution)/shard_map/pallas_call | solution.py:259
  26.7 9.6 %all_to_all.19 = f32[32,1,768]{2,1,0:T(1,128)S(1)} all-to-all(f32[32,1,768]{2,1,0:T(1,128)S(1)} %bitcast.9), channel_id=1, replica_groups=mesh['line'=4,'plane'=4,'narrow'=2] {'plane','line','narrow'}, dimensions={0} | all-to-all | bytes 196608 | tf_op jit(solution)/shard_map/all_to_all | solution.py:316
  36.3 0.8 %shard_map.52 = (f32[16,1024]{1,0:T(8,128)}, f32[16,16]{1,0:T(8,128)}) custom-call(f32[192,128]{1,0:T(8,128)S(1)} %bitcast.8), custom_call_target="tpu_custom_call" | custom-call | tf_op jit(solution)/shard_map/pallas_call | solution.py:303

commit v12 on v10

--- a/solution.py
+++ b/solution.py
@@ -63,7 +63,7 @@
     return steps
 
 
-def fetch_blocks(x_hbm, signs_hbm, x_ref, signs_ref, spread_ref, arrived, *others):
+def fetch_blocks(x_hbm, signs_hbm, x_ref, signs_ref, spread_ref, arrived, *others, meanwhile=None):
     columns, blocks = x_ref.shape[0], x_ref.shape[1] // LANES
     fetches = [
         pltpu.make_async_copy(x_hbm, x_ref, arrived.at[0]),
@@ -76,6 +76,8 @@
     signs = signs_ref[...].astype(jnp.float32)
     for block in range(blocks):
         spread_ref[block] = jnp.broadcast_to(signs[block : block + 1], (SUBLANES, LANES))
+    if meanwhile:
+        meanwhile()
     fetches[0].wait()
     signed = []
     for block in range(blocks):
@@ -98,19 +100,24 @@
     x_hbm, signs_hbm, samples_hbm, final_ref, out_ref, x_ref, signs_ref, spread_ref, samples_ref, arrived, noted
 ):
     note = pltpu.make_async_copy(samples_hbm, samples_ref, noted)
-    mixed = fetch_blocks(x_hbm, signs_hbm, x_ref, signs_ref, spread_ref, arrived, note)
     blocks, columns, _ = out_ref.shape
     slices = blocks // 2
     rows = final_ref.shape[0] // slices
-    note.wait()
-    samples = samples_ref[...].astype(jnp.float32)
-    per_row = slices // samples.shape[0]
-    for turn in range(per_row):
-        shift = LANES - turn * LANES // per_row
-        turned = pltpu.roll(samples, shift, 1) if turn else samples
-        for index in range(turn, slices, per_row):
-            tail = (index + 1) * rows - 1
-            final_ref[tail : tail + 1, :] = turned[index // per_row : index // per_row + 1]
+
+    def place_offsets():
+        note.wait()
+        samples = samples_ref[...].astype(jnp.float32)
+        per_row = slices // samples.shape[0]
+        for turn in range(per_row):
+            shift = LANES - turn * LANES // per_row
+            turned = pltpu.roll(samples, shift, 1) if turn else samples
+            for index in range(turn, slices, per_row):
+                tail = (index + 1) * rows - 1
+                final_ref[tail : tail + 1, :] = turned[index // per_row : index // per_row + 1]
+
+    mixed = fetch_blocks(
+        x_hbm, signs_hbm, x_ref, signs_ref, spread_ref, arrived, note, meanwhile=place_offsets
+    )
     steps = butterfly_steps(blocks)
     last = steps[-1][0]
     for apart, places in steps:

time: 36.6 us -> 36.6 us (level)
  no operation moved by 1% of the time
where the time goes in v12:
time: 36.6 us; the launch traced here: 36.4 us
  blocking collectives  32.8 us (90%)
  Pallas kernels  2.96 us (8%)
  between operations  0.65 us (2%)
    all_to_all x2, blocking collectives, exchange(): return lax.all_to_all(values, axes, split_axis=0, concat_axis=0, tiled=True)  32.8 us
    pallas_call x1, Pallas kernels, sliced_transform(): pl.pallas_call(sliced_kernel, out_shape=jax.ShapeDtypeStruct((blocks // 2...  1.5 us
    pallas_call x1, Pallas kernels, finish(): pl.pallas_call(finish_kernel, out_shape=(jax.ShapeDtypeStruct((columns, s...  0.79 us

profile of v12, /device:TPU:0, one launch (start us, length us, event | category | flops | bytes accessed | tf_op | source)
XLA Modules:
  0.0 36.4 jit_solution(8791713166035293731)
XLA Ops:
  0.6 1.5 %shard_map.50 = f32[1056,128]{1,0:T(8,128)S(1)} custom-call(f32[16,8192]{1,0:T(8,128)} %x_hbm.1, s32[64,128]{1,0:T(8,128)} %bitcast.10, s32[8,128]{1,0:T(8,128)} %bitcast.11), custom_call_target="tpu_custom_call" | custom-call | tf_op jit(solution)/shard_map/pallas_call | solution.py:169
  2.1 23.2 %all_to_all.18 = f32[32,1,4224]{2,1,0:T(1,128)S(1)} all-to-all(f32[32,1,4224]{2,1,0:T(1,128)S(1)} %bitcast.7), channel_id=1, replica_groups=mesh['line'=4,'plane'=4,'narrow'=2] {'plane','narrow','line'}, dimensions={0} | all-to-all | bytes 1081344 | tf_op jit(solution)/shard_map/all_to_all | solution.py:327
  25.3 0.7 %shard_map.51 = f32[192,128]{1,0:T(8,128)S(1)} custom-call(f32[1056,128]{1,0:T(8,128)S(1)} %bitcast.6), custom_call_target="tpu_custom_call" | custom-call | tf_op jit(solution)/shard_map/pallas_call | solution.py:270
  26.0 9.6 %all_to_all.19 = f32[32,1,768]{2,1,0:T(1,128)S(1)} all-to-all(f32[32,1,768]{2,1,0:T(1,128)S(1)} %bitcast.9), channel_id=1, replica_groups=mesh['line'=4,'plane'=4,'narrow'=2] {'plane','narrow','line'}, dimensions={0} | all-to-all | bytes 196608 | tf_op jit(solution)/shard_map/all_to_all | solution.py:327
  35.6 0.8 %shard_map.52 = (f32[16,1024]{1,0:T(8,128)}, f32[16,16]{1,0:T(8,128)}) custom-call(f32[192,128]{1,0:T(8,128)S(1)} %bitcast.8), custom_call_target="tpu_custom_call" | custom-call | tf_op jit(solution)/shard_map/pallas_call | solution.py:314
